TPU v7x, 256 devices: a whole 4x4x8 slice. The times are simulated.
256 devices in a mesh: scene: 8 (over y, core), blk: 32 (over x, z).
Axes of the slice: x: 4, y: 4, z: 8, core: 2. Of those that a mesh axis runs over, the one named last changes fastest.
Arguments:
- coarse_feat: bfloat16 [8, 128, 64, 256], P('scene', 'blk'), may hold values from -6 to 6
- coarse_nbr: int32 [8, 128, 4], P('scene', 'blk'), may hold values from -1 to 127, as said below
- fine_dest: int32 [8, 128], P('scene', 'blk'), may hold values from 0 to 127, as said below
- fine_nbr: int32 [8, 128, 4], P('scene', 'blk'), may hold values from -1 to 127, as said below
- skip: bfloat16 [8, 128, 512, 128], P('scene', 'blk'), may hold values from -12 to 12
- cotangent: bfloat16 [8, 128, 512, 128], P('scene', 'blk'), may hold values from -0.0078125 to 0.0078125
- w_coarse: bfloat16 [27, 256, 256], replicated, may hold values from -0.078125 to 0.078125
- w_up: bfloat16 [256, 128], replicated, may hold values from -0.375 to 0.375
- w_fine: bfloat16 [27, 128, 128], replicated, may hold values from -0.109375 to 0.109375
Outputs:
- fine_out: bfloat16 [8, 128, 512, 128], P('scene', 'blk')
- grad_fine: float32 [128, 27, 128], P('blk')
Inputs may be any that keep to these rules, and one draw needn't show every extreme that they name: `coarse_nbr`: entry k of coarse block b is the coarse index of the block beside b's face k, or -1. Neighbours are mutual, and lie on b's own device along blk or on the device just before or after it. `fine_dest`: for each scene a permutation of 0 to 127. Of the blocks that one device along blk holds in coarse order, at most 1 go to any one device along blk in fine order (fine index // 4), and that many do for some pair of devices. Entry k of fine block f is the fine index of the block beside f's face k, or -1; fine_nbr[s, fine_dest[s, b], k] = fine_dest[s, coarse_nbr[s, b, k]] where that entry is not -1, else -1. Neighbours lie on f's own device along blk or on the device just before or after it.
All inputs are finite; a program needn't handle non-finite values.
Results may differ from a plain program's by a relative error of at most 0.0058.
Values may be sent and summed in bfloat16 or wider, within the bound.
A program may use at most 64 MiB of HBM per device.

v0:
```python
import jax
import jax.numpy as jnp
from jax import lax
from jax.sharding import PartitionSpec as P

CEDGE = 4
FEDGE = 8


def with_halo(cells, sides, width):
    for axis, dim in sides:
        count = lax.axis_size(axis)
        ends = count - 1
        head = lax.slice_in_dim(cells, 0, width, axis=dim)
        tail = lax.slice_in_dim(cells, cells.shape[dim] - width, cells.shape[dim], axis=dim)
        cells = jnp.concatenate(
            [
                lax.ppermute(tail, axis, [(i, (i + 1) % count) for i in range(ends)]),
                cells,
                lax.ppermute(head, axis, [((i + 1) % count, i) for i in range(ends)]),
            ],
            axis=dim,
        )
    return cells


def upsample(block_cells, side_cells):
    block_count = block_cells.shape[0]
    channels = block_cells.shape[-1]
    cell_grid = block_cells.reshape(block_count, side_cells, side_cells, side_cells, channels)
    cell_grid = jnp.repeat(jnp.repeat(jnp.repeat(cell_grid, 2, axis=1), 2, axis=2), 2, axis=3)
    return cell_grid.reshape(block_count, 8 * side_cells**3, channels)


def facing_layers(cell_grid):
    return jnp.stack(
        [cell_grid[:, -1], cell_grid[:, 0], cell_grid[:, :, -1], cell_grid[:, :, 0]], axis=1
    )


def pad_faces(cell_grid, layers):
    padded = jnp.pad(cell_grid, ((0, 0), (1, 1), (1, 1), (1, 1), (0, 0)))
    padded = padded.at[:, 0, 1:-1, 1:-1].set(layers[:, 0])
    padded = padded.at[:, -1, 1:-1, 1:-1].set(layers[:, 1])
    padded = padded.at[:, 1:-1, 0, 1:-1].set(layers[:, 2])
    padded = padded.at[:, 1:-1, -1, 1:-1].set(layers[:, 3])
    return padded


def neighbour_layers(extended, face_table, first_index):
    row_count = extended.shape[0]
    block_count = face_table.shape[0]
    relative = face_table - first_index
    positions = jnp.arange(row_count, dtype=jnp.int32)
    chosen = []
    for face_index in range(4):
        selector = (
            (relative[:, face_index][:, None] == positions[None, :])
            & (face_table[:, face_index][:, None] >= 0)
        ).astype(jnp.bfloat16)
        flattened = extended[:, face_index].reshape(row_count, -1)
        fetched = jnp.dot(selector, flattened, preferred_element_type=jnp.float32).astype(
            jnp.bfloat16
        )
        chosen.append(fetched.reshape((block_count,) + extended.shape[2:]))
    return jnp.stack(chosen, axis=1)


def convolve(padded, weight, side_cells):
    block_count = padded.shape[0]
    channels = padded.shape[-1]
    running = None
    for off_x in range(3):
        for off_y in range(3):
            stacked = jnp.concatenate(
                [
                    padded[
                        :,
                        off_x : off_x + side_cells,
                        off_y : off_y + side_cells,
                        off_z : off_z + side_cells,
                    ]
                    for off_z in range(3)
                ],
                axis=-1,
            ).reshape(block_count * side_cells**3, 3 * channels)
            first_tap = 9 * off_x + 3 * off_y
            product = jnp.dot(
                stacked,
                weight[first_tap : first_tap + 3].reshape(3 * channels, -1),
                preferred_element_type=jnp.float32,
            )
            running = product if running is None else running + product
    return running


def silu_slope(pre_value):
    sigmoid_value = jax.nn.sigmoid(pre_value)
    return sigmoid_value * (1.0 + pre_value * (1.0 - sigmoid_value))


def body(coarse_feat, coarse_nbr, fine_dest, fine_nbr, skip, cotangent, w_coarse, w_up, w_fine):
    blocks = coarse_feat.shape[1]
    fine_chans = w_fine.shape[-1]
    peer_count = lax.axis_size("blk")
    repeats = (blocks + peer_count - 1) // peer_count
    position = lax.axis_index("blk")
    first_index = (position - 1) * blocks
    own_blocks = position * blocks + jnp.arange(blocks, dtype=jnp.int32)
    slot_index = jnp.arange(peer_count * repeats, dtype=jnp.int32)
    earlier = (
        jnp.arange(blocks, dtype=jnp.int32)[:, None] < jnp.arange(blocks, dtype=jnp.int32)[None, :]
    )
    coarse_grid = coarse_feat[0].reshape(blocks, CEDGE, CEDGE, CEDGE, -1)
    coarse_ext = with_halo(facing_layers(coarse_grid), (("blk", 0),), blocks)
    coarse_padded = pad_faces(coarse_grid, neighbour_layers(coarse_ext, coarse_nbr[0], first_index))
    coarse_act = jax.nn.silu(convolve(coarse_padded, w_coarse, CEDGE)).astype(jnp.bfloat16)
    projected = jnp.dot(coarse_act, w_up, preferred_element_type=jnp.float32).astype(jnp.bfloat16)
    projected = projected.reshape(blocks, CEDGE**3, fine_chans)
    target = fine_dest[0]
    owners = target // blocks
    same_owner = owners[:, None] == owners[None, :]
    rank = jnp.sum((same_owner & earlier).astype(jnp.int32), axis=0)
    slot_of = owners * repeats + rank
    to_slot = slot_of[None, :] == slot_index[:, None]
    labels = jnp.max(jnp.where(to_slot, target[None, :], -1), axis=1)
    weights_send = to_slot.astype(jnp.bfloat16)
    packed = jnp.dot(
        weights_send,
        upsample(projected, CEDGE).reshape(blocks, -1),
        preferred_element_type=jnp.float32,
    ).astype(jnp.bfloat16)
    arrived = lax.all_to_all(packed, "blk", split_axis=0, concat_axis=0, tiled=True)
    sources = lax.all_to_all(labels, "blk", split_axis=0, concat_axis=0, tiled=True)
    matches = (sources[None, :] == own_blocks[:, None]).astype(jnp.bfloat16)
    placed = jnp.dot(matches, arrived, preferred_element_type=jnp.float32).astype(jnp.bfloat16)
    fine_up = placed.reshape(blocks, FEDGE**3, fine_chans)
    hidden = (fine_up.astype(jnp.float32) + skip[0].astype(jnp.float32)).astype(jnp.bfloat16)
    fine_grid = hidden.reshape(blocks, FEDGE, FEDGE, FEDGE, fine_chans)
    fine_ext = with_halo(facing_layers(fine_grid), (("blk", 0),), blocks)
    fine_padded = pad_faces(fine_grid, neighbour_layers(fine_ext, fine_nbr[0], first_index))
    pre_fine = convolve(fine_padded, w_fine, FEDGE)
    outputs = [jax.nn.silu(pre_fine).astype(jnp.bfloat16).reshape(blocks, FEDGE**3, fine_chans)]
    delta_fine = (
        cotangent[0].reshape(-1, fine_chans).astype(jnp.float32) * silu_slope(pre_fine)
    ).astype(jnp.bfloat16)
    fine_out = jnp.stack(outputs)
    shard_rows = fine_chans // peer_count
    fine_padded, delta_fine = (fine_padded, delta_fine)
    tap_terms = []
    for off_x in range(3):
        for off_y in range(3):
            for off_z in range(3):
                piece = fine_padded[
                    :, off_x : off_x + FEDGE, off_y : off_y + FEDGE, off_z : off_z + FEDGE
                ].reshape(-1, fine_chans)
                tap_terms.append(
                    lax.dot_general(
                        piece,
                        delta_fine,
                        (((0,), (0,)), ((), ())),
                        preferred_element_type=jnp.float32,
                    )
                )
    running = jnp.stack(tap_terms, axis=1)
    summed = lax.psum(running, ("scene", "blk"))
    gradient = lax.dynamic_slice_in_dim(summed, position * shard_rows, shard_rows, 0)
    return (fine_out, gradient)


def solution(mesh):
    in_specs = (
        P("scene", "blk", None, None),
        P("scene", "blk", None),
        P("scene", "blk"),
        P("scene", "blk", None),
        P("scene", "blk", None, None),
        P("scene", "blk", None, None),
        P(),
        P(),
        P(),
    )
    out_specs = (P("scene", "blk", None, None), P("blk", None, None))
    return jax.shard_map(body, mesh=mesh, in_specs=in_specs, out_specs=out_specs, check_vma=False)
```

profile of v0, /device:TPU:1, one launch (start us, length us, event | category | flops | bytes accessed | tf_op | source)
XLA Modules:
  0.0 549.4 jit_solution(13759486911065288850)
XLA Ops:
  7.2 1.0 reshape_squeeze.28
  9.6 1.3 collective-permute-start.1
  10.9 5.7 %collective-permute-start = (bf16[4,4,4,4,256]{4,3,2,0,1:T(4,128)(2,1)}, bf16[4,4,4,4,256]{4,3,2,0,1:T(4,128)(2,1)}, u32[]{:S(2)}, u32[]{:S(2)}) collective-permute-start(bf16[4,4,4,4,256]{4,3,2,0,1:T(4,128)(2,1)} %pad_maximum_fusion.21), channel_id=1, source_target_pairs={{0,1},{1,2},{2,3},{3,4},{4,5},{5,6},{6,7},{7,8},{8,9},{9,10},{10,1... | collective-permute-start | bytes 393224 | tf_op jit(solution)/shard_map/ppermute | solution.py:18
  20.6 11.0 %all-to-all-start = ((s32[32,1,1]{2,1,0:T(1,128)}), s32[32,1,1]{2,1,0:T(1,128)S(1)}, u32[]{:S(2)}, u32[]{:S(2)}) async-start(s32[32,1,1]{2,1,0:T(1,128)} %copy.71), calls=%async_computation | async-start | bytes 32768 | tf_op jit(solution)/shard_map/all_to_all | solution.py:134
  31.7 3.1 fusion.88
  36.2 1.6 fusion.53
  37.9 1.4 pad_maximum_fusion.10
  39.2 0.8 fusion.95
  40.1 1.6 reshape_squeeze.29
  41.7 1.7 convolution_convert_fusion.9
  43.4 0.8 reshape.605
  44.2 1.6 reshape_squeeze.30
  45.8 1.7 convolution_convert_fusion.8
  47.5 1.4 reshape.606
  48.9 1.6 reshape_squeeze.31
  50.5 1.7 convolution_convert_fusion.7
  52.3 1.4 reshape.607
  54.4 1.1 convolution_convert_fusion.6
  55.8 0.9 scatter.29
  56.7 0.9 scatter.30
  58.0 1.1 fusion.94
  59.1 2.3 fusion.93
  61.6 0.8 reshape.609
  62.4 1.2 pad_maximum_fusion.12
  63.6 0.8 reshape.611
  64.5 1.1 pad_maximum_fusion.13
  65.6 0.9 reshape.613
  66.5 1.2 pad_maximum_fusion.14
  67.7 0.8 reshape.615
  68.6 1.2 pad_maximum_fusion.15
  69.8 0.9 reshape.617
  70.7 1.1 pad_maximum_fusion.16
  71.8 0.8 reshape.619
  72.6 1.2 pad_maximum_fusion.17
  73.9 0.9 reshape.621
  74.7 2.0 pad_maximum_fusion.18
  76.7 1.8 reshape.623
  78.6 1.8 pad_maximum_fusion.19
  80.4 1.8 reshape.625
  82.2 1.3 fusion.96
  83.6 1.3 convolution_add_fusion.15
  88.4 3.3 fusion
  92.2 6.8 %reduce.49 = bf16[32,65536]{1,0:T(8,128)(2,1)} reduce(bf16[32,1,65536]{2,0,1:T(8,128)(2,1)} %fusion, bf16[]{:T(256)} %broadcast.212), dimensions={1}, to_apply=%copy.79.reduce_sub_computation | reduce | bytes 8388610 | tf_op jit(solution)/shard_map/all_to_all | solution.py:133
  99.0 6.6 %reshape.698 = bf16[32,2,32768]{2,1,0:T(2,128)(2,1)} reshape(bf16[32,65536]{1,0:T(8,128)(2,1)} %reduce.49) | data formatting | bytes 8388608
  105.6 9.5 %all-to-all-start.1 = ((bf16[32,2,32768]{2,1,0:T(2,128)(2,1)}), bf16[32,2,32768]{2,1,0:T(2,128)(2,1)}, u32[]{:S(2)}, u32[]{:S(2)}) async-start(bf16[32,2,32768]{2,1,0:T(2,128)(2,1)} %reshape.698), calls=%async_computation.1 | async-start | bytes 8388608 | tf_op jit(solution)/shard_map/all_to_all | solution.py:133
  116.6 95.0 %all-to-all-done.1 = bf16[32,2,32768]{2,1,0:T(2,128)(2,1)} async-done(((bf16[32,2,32768]{2,1,0:T(2,128)(2,1)}), bf16[32,2,32768]{2,1,0:T(2,128)(2,1)}, u32[]{:S(2)}, u32[]{:S(2)}) %all-to-all-start.1) | async-done | bytes 4194336 | tf_op jit(solution)/shard_map/all_to_all | solution.py:133
  211.6 20.0 %reshape.699 = bf16[32,1,65536]{2,1,0:T(2,128)(2,1)} reshape(bf16[32,2,32768]{2,1,0:T(2,128)(2,1)} %all-to-all-done.1) | data formatting | bytes 8388608
  231.6 7.9 %fusion.4 = f32[1,4,512,128]{3,1,2,0:T(4,128)S(1)} fusion(bf16[32,1,65536]{2,1,0:T(2,128)(2,1)} %reshape.699, s32[32]{0:T(128)S(1)} %reduce.16, s32[4]{0:T(128)S(1)} %iota_add_fusion), kind=kOutput, calls=%fused_computation.31 | convolution fusion | flops 17301632 | bytes 5243024 | tf_op jit(solution)/shard_map/dot_general | solution.py:136
  239.7 0.9 copy-done.14
  240.9 1.3 collective-permute-start.3
  242.2 4.0 collective-permute-start.2
  246.2 0.8 slice_reduce_fusion
  248.1 0.9 collective-permute-done.3
  249.0 0.9 collective-permute-done.2
  250.3 0.9 fusion.7
  251.4 0.9 fusion.8
  252.4 0.8 fusion.9
  253.4 0.9 fusion.10
  255.3 0.9 fusion.90
  256.2 3.0 fusion.89
  266.9 1.7 fusion.38
  278.1 1.2 copy-done.2
  279.3 261.6 %all-reduce.4.cloned.1.call-done = f32[128,27,128]{2,0,1:T(8,128)} async-done(((f32[128,27,128]{2,0,1:T(8,128)}), f32[128,27,128]{2,0,1:T(8,128)}) %all-reduce.4.cloned.1.call-update) | async-done | bytes 1769488 | tf_op jit(solution)/shard_map/psum | solution.py:166
  540.9 1.5 constant_dynamic-slice_fusion
  (168 shorter events, 33.7 us)
Async XLA Ops:
  7.2 79.7 %copy-start = (bf16[256,128]{1,0:T(8,128)(2,1)S(1)}, bf16[256,128]{1,0:T(8,128)(2,1)}, u32[]{:S(2)}) copy-start(bf16[256,128]{1,0:T(8,128)(2,1)} %param.32) | copy-start | bytes 196612
  8.2 0.6 copy-start.17
  8.2 1.4 copy-start.18
  8.2 2.6 copy-start.19
  8.3 8.3 %copy-start.20 = (bf16[4,1,4,4,256]{4,3,2,0,1:T(4,128)(2,1)}, bf16[4,1,4,4,256]{4,3,2,0,1:T(4,128)(2,1)S(1)}, u32[]{:S(2)}) copy-start(bf16[4,1,4,4,256]{4,3,2,0,1:T(4,128)(2,1)S(1)} %get-tuple-element.201) | copy-start | bytes 98308
  9.6 28.3 %collective-permute-start.1 = (bf16[4,4,4,4,256]{4,3,2,0,1:T(4,128)(2,1)}, bf16[4,4,4,4,256]{4,3,2,0,1:T(4,128)(2,1)}, u32[]{:S(2)}, u32[]{:S(2)}) collective-permute-start(bf16[4,4,4,4,256]{4,3,2,0,1:T(4,128)(2,1)} %pad_maximum_fusion.21), channel_id=1, source_target_pairs={{1,0},{2,1},{3,2},{4,3},{5,4},{6,5},{7,6},{8,7},{9,8},{10,9},{11,1... | collective-permute-start | bytes 393224 | tf_op jit(solution)/shard_map/ppermute | solution.py:20
  10.9 27.0 %collective-permute-start = (bf16[4,4,4,4,256]{4,3,2,0,1:T(4,128)(2,1)}, bf16[4,4,4,4,256]{4,3,2,0,1:T(4,128)(2,1)}, u32[]{:S(2)}, u32[]{:S(2)}) collective-permute-start(bf16[4,4,4,4,256]{4,3,2,0,1:T(4,128)(2,1)} %pad_maximum_fusion.21), channel_id=1, source_target_pairs={{0,1},{1,2},{2,3},{3,4},{4,5},{5,6},{6,7},{7,8},{8,9},{9,10},{10,1... | collective-permute-start | bytes 393224 | tf_op jit(solution)/shard_map/ppermute | solution.py:18
  18.6 0.6 copy-start.30
  20.6 84.9 %all-to-all-start = ((s32[32,1,1]{2,1,0:T(1,128)}), s32[32,1,1]{2,1,0:T(1,128)S(1)}, u32[]{:S(2)}, u32[]{:S(2)}) async-start(s32[32,1,1]{2,1,0:T(1,128)} %copy.71), calls=%async_computation | async-start | bytes 32768 | tf_op jit(solution)/shard_map/all_to_all | solution.py:134
  31.6 3.1 copy-start.22
  31.7 3.1 copy-start.23
  36.2 5.5 copy-start.32
  61.4 3.1 copy-start.13
  66.5 4.2 copy-start.12
  72.6 6.0 %copy-start.11 = (bf16[4,4,4,4,256]{4,3,2,1,0:T(4,128)(2,1)S(1)}, bf16[4,4,4,4,256]{4,3,2,1,0:T(4,128)(2,1)}, u32[]{:S(2)}) copy-start(bf16[4,4,4,4,256]{4,3,2,1,0:T(4,128)(2,1)} %get-tuple-element.166) | copy-start | bytes 393220
  74.7 7.5 %copy-start.3 = (bf16[3,256,256]{2,1,0:T(8,128)(2,1)S(1)}, bf16[3,256,256]{2,1,0:T(8,128)(2,1)}, u32[]{:S(2)}) copy-start(bf16[3,256,256]{2,1,0:T(8,128)(2,1)} %get-tuple-element.121) | copy-start | bytes 1179652
  82.2 2.7 copy-start.4
  82.2 3.0 copy-start.5
  83.6 1.9 copy-start.6
  84.9 1.0 copy-start.7
  85.2 1.0 copy-start.8
  85.5 1.1 copy-start.9
  85.9 1.0 copy-start.15
  85.9 1.1 copy-start.16
  87.0 1.3 copy-start.31
  105.6 9.6 %copy-start.24 = (s32[1,4,4]{2,1,0:T(4,128)S(1)}, s32[1,4,4]{2,1,0:T(4,128)}, u32[]{:S(2)}) copy-start(s32[1,4,4]{2,1,0:T(4,128)} %param.28) | copy-start | bytes 196
  105.6 106.0 %all-to-all-start.1 = ((bf16[32,2,32768]{2,1,0:T(2,128)(2,1)}), bf16[32,2,32768]{2,1,0:T(2,128)(2,1)}, u32[]{:S(2)}, u32[]{:S(2)}) async-start(bf16[32,2,32768]{2,1,0:T(2,128)(2,1)} %reshape.698), calls=%async_computation.1 | async-start | bytes 8388608 | tf_op jit(solution)/shard_map/all_to_all | solution.py:133
  115.1 425.8 %all-reduce.4.cloned.1.call-start = ((), (), s32[]{:S(2)}) async-start(), calls=%async_computation.2 | async-start | bytes 3538944 | tf_op jit(solution)/shard_map/psum | solution.py:166
  239.6 1.0 copy-start.14
  239.7 6.5 %copy-start.25 = (s32[4,4]{1,0:T(4,128)S(1)}, s32[4,4]{1,0:T(4,128)}, u32[]{:S(2)}) copy-start(s32[4,4]{1,0:T(4,128)} %get-tuple-element.204) | copy-start | bytes 196
  239.7 7.3 %copy-start.10 = (bf16[27,128,128]{2,1,0:T(8,128)(2,1)S(1)}, bf16[27,128,128]{2,1,0:T(8,128)(2,1)}, u32[]{:S(2)}) copy-start(bf16[27,128,128]{2,1,0:T(8,128)(2,1)} %param.33) | copy-start | bytes 2654212
  240.9 8.1 %collective-permute-start.3 = (bf16[4,4,8,8,128]{4,3,2,0,1:T(8,128)(2,1)S(1)}, bf16[4,4,8,8,128]{4,3,2,0,1:T(8,128)(2,1)S(1)}, u32[]{:S(2)}, u32[]{:S(2)}) collective-permute-start(bf16[4,4,8,8,128]{4,3,2,0,1:T(8,128)(2,1)S(1)} %pad_maximum_fusion.20), channel_id=1, source_target_pairs={{1,0},{2,1},{3,2},{4,3},{5,4},{6,5},{7,6},{8,7},{9,8},{10,9},{11,1... | collective-permute-start | bytes 786440 | tf_op jit(solution)/shard_map/ppermute | solution.py:20
  242.2 7.7 %collective-permute-start.2 = (bf16[4,4,8,8,128]{4,3,2,0,1:T(8,128)(2,1)S(1)}, bf16[4,4,8,8,128]{4,3,2,0,1:T(8,128)(2,1)S(1)}, u32[]{:S(2)}, u32[]{:S(2)}) collective-permute-start(bf16[4,4,8,8,128]{4,3,2,0,1:T(8,128)(2,1)S(1)} %pad_maximum_fusion.20), channel_id=1, source_target_pairs={{0,1},{1,2},{2,3},{3,4},{4,5},{5,6},{6,7},{7,8},{8,9},{9,10},{10,1... | collective-permute-start | bytes 786440 | tf_op jit(solution)/shard_map/ppermute | solution.py:18
  248.1 2.2 copy-start.29
  250.0 1.3 copy-start.28
  250.0 2.4 copy-start.27
  250.1 3.3 copy-start.26
  265.8 0.9 copy-start.21
  265.8 1.1 copy-start.33
  277.4 265.0 %copy-start.1 = (bf16[256,128]{1,0:T(8,128)(2,1)S(1)}, bf16[256,128]{1,0:T(8,128)(2,1)}, u32[]{:S(2)}) copy-start(bf16[256,128]{1,0:T(8,128)(2,1)} %param.32) | copy-start | bytes 196612
  278.1 1.2 copy-start.2
Sparse Core Ops, SparseCore 0:
  279.4 261.3 all-reduce.3
where the time goes:
time: 555 us; the launch traced here: 549 us
  waiting for transfers between devices  358 us (65%)
  local copies, waits for them, and re-layouts  72.7 us (13%)
  matrix products  41.4 us (7%)
  starting transfers between devices  32.8 us (6%)
  other arithmetic  28.9 us (5%)
  between operations  15.2 us (3%)
    psum x1, waiting for transfers between devices, body(): summed = lax.psum(running, ('scene', 'blk'))  262 us
    all_to_all x1, waiting for transfers between devices, body(): lax.all_to_all(packed, 'blk', split_axis=0, concat_axis=0, tiled=True)  95 us
    unnamed x77, local copies, waits for them, and re-layouts  31.4 us
    concatenate x18, other arithmetic, convolve(): jnp.concatenate([padded[:, off_x:off_x + side_cells, off_y:off_y + side_c...  13.2 us
  transfers between devices with their start and end apart: 7, of which 4 were waited for; matrix products, arithmetic and copies ran while one was open for 15% of the time, Pallas kernels for 0%

commit v1 on v0

v1 whole, which is shorter than its diff:
```python
import functools

import jax
import jax.numpy as jnp
import numpy as np
from jax import lax
from jax.experimental import pallas as pl
from jax.experimental.pallas import tpu as pltpu
from jax.sharding import PartitionSpec as P

MESH = pl.DeviceIdType.MESH
BLOCKS = 4
LINES = 16
TAPS = 27
CF = 128
CC = 256
BF16 = jnp.bfloat16
F32 = jnp.float32


def coarse_selector():
    rows = np.zeros((3, 3, 6, 4, 4, 256), np.float32)
    for q, r, px, y, z in np.ndindex(3, 3, 6, 4, 4):
        x, yy, zz = px - 1, y + q - 1, z + r - 1
        if not 0 <= zz < 4:
            continue
        inside = 0 <= yy < 4
        if x == -1 or x == 4:
            if inside:
                rows[q, r, px, y, z, (192 if x == -1 else 208) + 4 * yy + zz] = 1
        elif inside:
            rows[q, r, px, y, z, 16 * x + 4 * yy + zz] = 1
        elif yy == -1:
            rows[q, r, px, y, z, 64 + 16 * x + 12 + zz] = 1
        else:
            rows[q, r, px, y, z, 128 + 16 * x + zz] = 1
    return rows.reshape(864, 256)


def line_order():
    order = np.arange(256).reshape(BLOCKS, LINES, 4).transpose(1, 0, 2).reshape(-1)
    return np.eye(256, dtype=np.float32)[order]


def doubled_rows():
    source = (np.arange(12)[:, None] * 4 + np.arange(8)[None, :] // 2).reshape(-1)
    return np.eye(48, dtype=np.float32)[source]


def shard_order(taps):
    order = np.arange(taps * CF).reshape(taps, CF).T.reshape(-1)
    return np.eye(taps * CF, dtype=np.float32)[order]


def kernel(
    n_blk,
    n_scene,
    group,
    feat,
    coarse_nbr,
    dest,
    fine_nbr,
    skip,
    cot,
    w_coarse,
    w_up,
    w_fine,
    sel_c,
    order_c,
    double_z,
    order_g,
    out,
    grad,
    ext,
    wc,
    wu,
    wf,
    skip_v,
    cot_v,
    sel_cv,
    order_cv,
    double_v,
    order_gv,
    cols_c,
    meta_src,
    meta,
    line_src,
    lines,
    sel,
    perm,
    got,
    up,
    faces,
    cols,
    delta_t,
    out_v,
    pair_src,
    pair_dst,
    y_src,
    y_dst,
    shard_src,
    shards,
    done_src,
    done,
    local_sem,
    halo_send,
    halo_recv,
    meta_send,
    meta_recv,
    line_send,
    line_recv,
    got_send,
    got_recv,
    pair_send,
    pair_recv,
    y_send,
    y_recv,
    shard_send,
    shard_recv,
    done_send,
    done_recv,
    out_sem,
):
    me = lax.axis_index("blk")
    scene = lax.axis_index("scene")
    core = lax.rem(scene, 2)
    row = scene // 2
    rows = n_scene // 2
    stride = n_blk // LINES
    odd = lax.rem(scene, stride)
    right = lax.rem(me + 1, n_blk)
    left = lax.rem(me + n_blk - 1, n_blk)
    is_mid = lax.rem(me, stride) == odd

    loads = [
        pltpu.make_async_copy(source, target, local_sem.at[index])
        for index, (source, target) in enumerate(
            (
                (feat.at[0], ext.at[pl.ds(BLOCKS, BLOCKS)]),
                (skip.at[0], skip_v),
                (sel_c, sel_cv),
                (w_coarse, wc),
                (w_up, wu),
                (order_c, order_cv),
                (double_z, double_v),
                (w_fine, wf),
                (cot.at[0], cot_v),
                (order_g, order_gv),
            )
        )
    ]
    for load in loads:
        load.start()
    (
        load_feat,
        load_skip,
        load_sel,
        load_wc,
        load_wu,
        load_order,
        load_double,
        load_wf,
        load_cot,
        load_gorder,
    ) = loads

    barrier = pltpu.get_barrier_semaphore()

    def greet_blk(k, carry):
        pl.semaphore_signal(
            barrier,
            inc=1,
            device_id={"blk": lax.rem(me + k, n_blk)},
            device_id_type=MESH,
        )
        return carry

    def greet_scene(k, carry):
        pl.semaphore_signal(
            barrier,
            inc=1,
            device_id={"scene": lax.rem(scene + k, n_scene)},
            device_id_type=MESH,
        )
        return carry

    lax.fori_loop(1, n_blk, greet_blk, 0)
    lax.fori_loop(1, n_scene, greet_scene, 0)

    message_row = lax.broadcasted_iota(jnp.int32, (16, CF), 0)
    owner_rows = lax.rem(message_row, 4)
    for b in range(BLOCKS):
        owner_rows = owner_rows + jnp.where(message_row // 4 == b, 4 * dest[0, b], 0)
    meta_src[...] = owner_rows

    pl.semaphore_wait(barrier, n_blk + n_scene - 2)

    def remote(source, target, send, recv, **where):
        return pltpu.make_async_remote_copy(
            src_ref=source,
            dst_ref=target,
            send_sem=send,
            recv_sem=recv,
            device_id=where,
            device_id_type=MESH,
        )

    feat_right = remote(
        feat.at[0], ext.at[pl.ds(0, BLOCKS)], halo_send.at[0], halo_recv.at[0], blk=right
    )
    feat_left = remote(
        feat.at[0], ext.at[pl.ds(2 * BLOCKS, BLOCKS)], halo_send.at[1], halo_recv.at[1], blk=left
    )
    feat_right.start()
    feat_left.start()

    def over_lines(action):
        def step(k, carry):
            line = lax.rem(me // stride + k, LINES)
            action(line, line * stride + odd)
            return carry

        lax.fori_loop(0, LINES, step, 0)

    def meta_copy(line, peer):
        return remote(meta_src, meta.at[me], meta_send.at[line], meta_recv, blk=peer)

    def send_meta(line, peer):
        @pl.when(peer == me)
        def _():
            pltpu.make_async_copy(meta_src, meta.at[me], meta_recv).start()

        @pl.when(peer != me)
        def _():
            meta_copy(line, peer).start()

    over_lines(send_meta)

    load_skip.wait()

    def gather_faces(b, carry):
        faces[BLOCKS + b, 0] = skip_v[b, pl.ds(448, 64)]
        faces[BLOCKS + b, 1] = skip_v[b, pl.ds(0, 64)]
        layers = [
            skip_v[b, pl.ds(64 * x, 64)].astype(F32).reshape(8, 8, CF) for x in range(8)
        ]
        for face, y in ((2, 7), (3, 0)):
            layer = jnp.concatenate([part[y] for part in layers], axis=0)
            faces[BLOCKS + b, face] = layer.astype(BF16)
        return carry

    lax.fori_loop(0, BLOCKS, gather_faces, 0)
    own_faces = faces.at[pl.ds(BLOCKS, BLOCKS)]
    faces_right = remote(
        own_faces, faces.at[pl.ds(0, BLOCKS)], halo_send.at[2], halo_recv.at[2], blk=right
    )
    faces_left = remote(
        own_faces, faces.at[pl.ds(2 * BLOCKS, BLOCKS)], halo_send.at[3], halo_recv.at[3], blk=left
    )
    faces_right.start()
    faces_left.start()

    first = (me - 1) * BLOCKS
    last_slot = 3 * BLOCKS - 1
    load_feat.wait()
    load_sel.wait()
    feat_right.wait_recv()
    feat_left.wait_recv()

    def coarse_columns(b, carry):
        def beside(face, start, size):
            index = coarse_nbr[0, b, face]
            slot = jnp.clip(index - first, 0, last_slot)
            values = ext[slot, pl.ds(start, size), :]
            return jnp.where(index >= 0, values, jnp.zeros_like(values))

        sources = jnp.concatenate(
            [
                ext[BLOCKS + b],
                beside(2, 0, 64),
                beside(3, 0, 64),
                beside(0, 48, 16),
                beside(1, 0, 16),
                jnp.zeros((32, CC), BF16),
            ],
            axis=0,
        )
        cols_c[b] = jnp.dot(sel_cv[...], sources, preferred_element_type=F32).astype(BF16)
        return carry

    lax.fori_loop(0, BLOCKS, coarse_columns, 0)
    load_wc.wait()
    coarse = None
    for p in range(3):
        left_side = jnp.concatenate(
            [
                cols_c[:, 96 * qr + 16 * p : 96 * qr + 16 * p + 64, :].reshape(256, CC)
                for qr in range(9)
            ],
            axis=1,
        )
        product = jnp.dot(
            left_side,
            wc[9 * p : 9 * p + 9].reshape(9 * CC, CC),
            preferred_element_type=F32,
        )
        coarse = product if coarse is None else coarse + product
    active = (coarse / (1.0 + jnp.exp(-coarse))).astype(BF16)
    load_wu.wait()
    load_order.wait()
    projected = jnp.dot(active, wu[...], preferred_element_type=F32).astype(BF16)
    line_src[...] = (
        jnp.dot(order_cv[...], projected, preferred_element_type=F32)
        .astype(BF16)
        .reshape(LINES, 16, CF)
    )

    def line_copy(line, peer):
        return remote(line_src.at[line], lines.at[me], line_send.at[line], line_recv, blk=peer)

    def send_line(line, peer):
        @pl.when(peer == me)
        def _():
            pltpu.make_async_copy(line_src.at[line], lines.at[me], line_recv).start()

        @pl.when(peer != me)
        def _():
            line_copy(line, peer).start()

    over_lines(send_line)

    total = n_blk * 16
    my_line = me // stride

    def owner_copy(peer):
        return remote(
            perm.at[pl.ds(16 * peer, 48)],
            got.at[my_line],
            got_send.at[peer],
            got_recv,
            blk=peer,
        )

    @pl.when(is_mid)
    def _():
        pltpu.make_async_copy(meta, meta, meta_recv).wait()
        wanted = meta[...].reshape(total, CF)
        lane = lax.broadcasted_iota(jnp.int32, (total, CF), 1)
        for part in range(total // CF):
            hit = jnp.where(wanted == lane + part * CF, 1.0, 0.0)
            sel[part * CF : (part + 1) * CF, :] = hit.T.astype(BF16)
        perm[0:16, :] = jnp.zeros((16, CF), BF16)
        perm[total + 16 : total + 32, :] = jnp.zeros((16, CF), BF16)
        pltpu.make_async_copy(lines, lines, line_recv).wait()
        perm[16 : total + 16, :] = jnp.dot(
            sel[...], lines[...].reshape(total, CF), preferred_element_type=F32
        ).astype(BF16)
        pltpu.make_async_copy(perm.at[pl.ds(16 * me, 48)], got.at[my_line], got_recv).start()

        def step(k, carry):
            owner_copy(lax.rem(me + k, n_blk)).start()
            return carry

        lax.fori_loop(1, n_blk, step, 0)

    load_double.wait()
    load_wf.wait()
    load_cot.wait()
    faces_right.wait_recv()
    faces_left.wait_recv()
    pltpu.make_async_copy(got, got, got_recv).wait()

    def double_lines(line, carry):
        up[line] = jnp.dot(
            double_v[...], got[line], preferred_element_type=F32
        ).reshape(12, 8, CF)
        return carry

    lax.fori_loop(0, LINES, double_lines, 0)

    def fine_block(b, carry):
        def beside(face):
            index = fine_nbr[0, b, face]
            slot = jnp.clip(index - first, 0, last_slot)
            skips = faces[slot, face].astype(F32).reshape(8, 8, CF)
            parts = []
            for step in range(8):
                half = step // 2
                line = (12 + half, half, 4 * half + 3, 4 * half)[face]
                parts.append(up[line, slot] + skips[step])
            layer = jnp.stack(parts, axis=0)
            return jnp.where(index >= 0, layer, jnp.zeros_like(layer))

        low_x, high_x, low_y, high_y = (beside(face) for face in range(4))
        edge = jnp.zeros((1, 8, CF), F32)
        z_index = lax.broadcasted_iota(jnp.int32, (10, 8, CF), 1)
        for px in range(10):
            if px == 0:
                layer = jnp.concatenate([edge, low_x, edge], axis=0)
            elif px == 9:
                layer = jnp.concatenate([edge, high_x, edge], axis=0)
            else:
                x = px - 1
                skips = skip_v[b, pl.ds(64 * x, 64)].astype(F32).reshape(8, 8, CF)
                own = [up[4 * (x // 2) + y // 2, BLOCKS + b] + skips[y] for y in range(8)]
                layer = jnp.stack([low_y[x]] + own + [high_y[x]], axis=0)
            shifted = (
                jnp.where(z_index == 0, 0.0, pltpu.roll(layer, 1, 1)),
                layer,
                jnp.where(z_index == 7, 0.0, pltpu.roll(layer, 7, 1)),
            )
            for q in range(3):
                for r in range(3):
                    cols[3 * q + r, b, px] = shifted[r][q : q + 8].reshape(64, CF).astype(BF16)
        pre = None
        for p in range(3):
            left_side = jnp.concatenate(
                [cols[qr, b, p : p + 8].reshape(512, CF) for qr in range(9)], axis=1
            )
            product = jnp.dot(
                left_side,
                wf[9 * p : 9 * p + 9].reshape(9 * CF, CF),
                preferred_element_type=F32,
            )
            pre = product if pre is None else pre + product
        sigma = 1.0 / (1.0 + jnp.exp(-pre))
        out_v[b] = (pre * sigma).astype(BF16)
        delta = cot_v[b].astype(F32) * (sigma * (1.0 + pre * (1.0 - sigma)))
        delta_t[b] = delta.T.astype(BF16)
        return carry

    lax.fori_loop(0, BLOCKS, fine_block, 0)
    write_out = pltpu.make_async_copy(out_v, out.at[0], out_sem)
    write_out.start()

    def group_terms(index):
        pairs = []
        for first_tap in range(0, group, 2):
            picked = []
            for tap in (first_tap, first_tap + 1):
                which = lax.rem(index * group + tap, TAPS)
                picked.append((which // 9, lax.rem(which, 9)))
            terms = None
            for b in range(BLOCKS):
                sides = jnp.concatenate(
                    [cols[qr, b, pl.ds(p, 8)].reshape(512, CF) for p, qr in picked], axis=1
                )
                product = jnp.dot(delta_t[b], sides, preferred_element_type=F32)
                terms = product if terms is None else terms + product
            pairs.append(terms)
        return jnp.concatenate(pairs, axis=1)

    def pair_copy(k):
        return remote(
            pair_src.at[k],
            pair_dst.at[k],
            pair_send.at[k],
            pair_recv.at[k],
            scene=scene + 1 - 2 * core,
        )

    def y_copy(k):
        return remote(
            y_src.at[k],
            y_dst.at[k],
            y_send.at[k],
            y_recv.at[k],
            scene=2 * lax.rem(row + 1 + k, rows) + core,
        )

    def for_partner(k, carry):
        pair_src[k] = group_terms(2 * lax.rem(row + 1 + k, rows) + 1 - core).astype(BF16)
        pair_copy(k).start()
        return carry

    lax.fori_loop(0, rows, for_partner, 0)

    def pair_sum(k):
        terms = group_terms(2 * lax.rem(row + 1 + k, rows) + core)
        pair_copy(k).wait_recv()
        return terms + pair_dst[k].astype(F32)

    def for_row(k, carry):
        y_src[k] = pair_sum(k).astype(BF16)
        y_copy(k).start()
        return carry

    lax.fori_loop(0, rows - 1, for_row, 0)
    scene_sum = pair_sum(rows - 1)
    for k in range(rows - 1):
        y_copy(k).wait_recv()
        scene_sum = scene_sum + y_dst[k].astype(F32)
    load_gorder.wait()
    ordered = lax.dot_general(
        order_gv[...],
        scene_sum.astype(BF16),
        (((1,), (1,)), ((), ())),
        preferred_element_type=F32,
    )
    shard_src[...] = ordered.astype(BF16).reshape(shard_src.shape)

    def shard_copy(k):
        peer = lax.rem(me + k, n_blk)
        return remote(
            shard_src.at[peer], shards.at[me], shard_send.at[peer], shard_recv, blk=peer
        )

    pltpu.make_async_copy(shard_src.at[me], shards.at[me], shard_recv).start()

    def send_shard(k, carry):
        shard_copy(k).start()
        return carry

    lax.fori_loop(1, n_blk, send_shard, 0)
    pltpu.make_async_copy(shards, shards, shard_recv).wait()
    done_src[...] = jnp.sum(shards[...].astype(F32), axis=0)

    def done_copy(k):
        peer = lax.rem(scene + k, n_scene)
        return remote(done_src, done.at[scene], done_send.at[peer], done_recv, scene=peer)

    pltpu.make_async_copy(done_src, done.at[scene], done_recv).start()

    def send_done(k, carry):
        done_copy(k).start()
        return carry

    lax.fori_loop(1, n_scene, send_done, 0)
    pltpu.make_async_copy(done, done, done_recv).wait()
    for index in range(n_scene):
        count = min(group, TAPS - index * group)
        if count <= 0:
            continue
        for channel in range(CF // n_blk):
            grad[channel, index * group : index * group + count, :] = done[
                index, channel * group : channel * group + count, :
            ]

    feat_right.wait_send()
    feat_left.wait_send()
    faces_right.wait_send()
    faces_left.wait_send()

    def sent_line(line, peer):
        @pl.when(peer != me)
        def _():
            meta_copy(line, peer).wait_send()
            line_copy(line, peer).wait_send()

    over_lines(sent_line)

    @pl.when(is_mid)
    def _():
        def step(k, carry):
            owner_copy(lax.rem(me + k, n_blk)).wait_send()
            return carry

        lax.fori_loop(1, n_blk, step, 0)

    for k in range(rows):
        pair_copy(k).wait_send()
    for k in range(rows - 1):
        y_copy(k).wait_send()

    def sent_shard(k, carry):
        shard_copy(k).wait_send()
        return carry

    lax.fori_loop(1, n_blk, sent_shard, 0)

    def sent_done(k, carry):
        done_copy(k).wait_send()
        return carry

    lax.fori_loop(1, n_scene, sent_done, 0)
    write_out.wait()


def body(n_blk, n_scene, feat, coarse_nbr, dest, fine_nbr, skip, cot, w_coarse, w_up, w_fine):
    group = 4 * -(-TAPS // (4 * n_scene))
    shard = CF // n_blk
    rows = n_scene // 2
    any_spec = pl.BlockSpec(memory_space=pl.ANY)
    smem_spec = pl.BlockSpec(memory_space=pltpu.SMEM)
    vmem_spec = pl.BlockSpec(memory_space=pltpu.VMEM)
    vmem = pltpu.VMEM
    dma = pltpu.SemaphoreType.DMA
    scratch = [
        vmem((3 * BLOCKS, 64, CC), BF16),
        vmem((TAPS, CC, CC), BF16),
        vmem((CC, CF), BF16),
        vmem((TAPS, CF, CF), BF16),
        vmem((BLOCKS, 512, CF), BF16),
        vmem((BLOCKS, 512, CF), BF16),
        vmem((864, 256), BF16),
        vmem((256, 256), BF16),
        vmem((96, 48), BF16),
        vmem((group * CF, group * CF), BF16),
        vmem((BLOCKS, 864, CC), BF16),
        vmem((16, CF), jnp.int32),
        vmem((n_blk, 16, CF), jnp.int32),
        vmem((LINES, 16, CF), BF16),
        vmem((n_blk, 16, CF), BF16),
        vmem((n_blk * 16, n_blk * 16), BF16),
        vmem((n_blk * 16 + 32, CF), BF16),
        vmem((LINES, 48, CF), BF16),
        vmem((LINES, 12, 8, CF), F32),
        vmem((3 * BLOCKS, 4, 64, CF), BF16),
        vmem((9, BLOCKS, 10, 64, CF), BF16),
        vmem((BLOCKS, CF, 512), BF16),
        vmem((BLOCKS, 512, CF), BF16),
        vmem((rows, CF, group * CF), BF16),
        vmem((rows, CF, group * CF), BF16),
        vmem((max(rows - 1, 1), CF, group * CF), BF16),
        vmem((max(rows - 1, 1), CF, group * CF), BF16),
        vmem((n_blk, shard * group, CF), BF16),
        vmem((n_blk, shard * group, CF), BF16),
        vmem((shard * group, CF), F32),
        vmem((n_scene, shard * group, CF), F32),
        dma((10,)),
        dma((4,)),
        dma((4,)),
        dma((LINES,)),
        dma,
        dma((LINES,)),
        dma,
        dma((n_blk,)),
        dma,
        dma((rows,)),
        dma((rows,)),
        dma((max(rows - 1, 1),)),
        dma((max(rows - 1, 1),)),
        dma((n_blk,)),
        dma,
        dma((n_scene,)),
        dma,
        dma,
    ]
    fine_out, gradient = pl.pallas_call(
        functools.partial(kernel, n_blk, n_scene, group),
        out_shape=(
            jax.ShapeDtypeStruct((1, BLOCKS, 512, CF), BF16),
            jax.ShapeDtypeStruct((shard, TAPS, CF), F32),
        ),
        in_specs=[any_spec, smem_spec, smem_spec, smem_spec] + [any_spec] * 9,
        out_specs=(any_spec, vmem_spec),
        scratch_shapes=scratch,
        compiler_params=pltpu.CompilerParams(
            collective_id=0, has_side_effects=True, vmem_limit_bytes=60 * 1024 * 1024
        ),
        name="decoder_level",
    )(
        feat,
        coarse_nbr,
        dest,
        fine_nbr,
        skip,
        cot,
        w_coarse,
        w_up,
        w_fine,
        jnp.asarray(coarse_selector(), BF16),
        jnp.asarray(line_order(), BF16),
        jnp.asarray(doubled_rows(), BF16),
        jnp.asarray(shard_order(group), BF16),
    )
    return fine_out, gradient


def solution(mesh):
    in_specs = (
        P("scene", "blk", None, None),
        P("scene", "blk", None),
        P("scene", "blk"),
        P("scene", "blk", None),
        P("scene", "blk", None, None),
        P("scene", "blk", None, None),
        P(),
        P(),
        P(),
    )
    out_specs = (P("scene", "blk", None, None), P("blk", None, None))
    return jax.shard_map(
        functools.partial(body, mesh.shape["blk"], mesh.shape["scene"]),
        mesh=mesh,
        in_specs=in_specs,
        out_specs=out_specs,
        check_vma=False,
    )
```

time: 555 us -> 72.7 us (0.13)
  waiting for transfers between devices: 358 us -> 0 us
  local copies, waits for them, and re-layouts: 72.7 us -> 3.37 us
  Pallas kernels: 0 us -> 68.5 us
  matrix products: 41.4 us -> 0 us
  starting transfers between devices: 32.8 us -> 0 us
  other arithmetic: 28.9 us -> 0 us
  between operations: 15.2 us -> 0.64 us
    psum x1 -> x0, waiting for transfers between devices: 262 us -> none  [body(): summed = lax.psum(running, ('scene', 'blk'))]
    all_to_all x2 -> x0, waiting for transfers between devices: 95 us -> none  [the longest x1 95 us: body(): lax.all_to_all(packed, 'blk', split_axis=0, concat_axis=0, tiled=True)]
    pallas_call x0 -> x1, Pallas kernels: none -> 68.5 us  [body(): pl.pallas_call(functools.partial(kernel, n_blk, n_scene, group), out_shap...]
    dot_general x55 -> x0, matrix products: 41.4 us -> none  [the longest x17 10.6 us: convolve(): jnp.dot(stacked, weight[first_tap:first_tap + 3].reshape(3 * channels, -1...]
    unnamed x77 -> x1, local copies, waits for them, and re-layouts: 31.4 us -> 1.87 us
    all_to_all x2 -> x0, starting transfers between devices: 20.5 us -> none  [the longest x1 11 us: body(): lax.all_to_all(labels, 'blk', split_axis=0, concat_axis=0, tiled=True)]
    concatenate x20 -> x0, other arithmetic: 14.7 us -> none  [the longest x18 13.2 us: convolve(): jnp.concatenate([padded[:, off_x:off_x + side_cells, off_y:off_y + side_c...]
    slice x10 -> x0, local copies, waits for them, and re-layouts: 13.6 us -> none  [the longest x4 7.35 us: convolve(): padded[:, off_x:off_x + side_cells, off_y:off_y + side_cells, off_z:off_z...]
  transfers between devices with their start and end apart: 7 -> 0, of which waited for: 4 -> 0; matrix products, arithmetic and copies ran while one was open for 15% -> 0% of each run, Pallas kernels for 0% -> 0%
where the time goes in v1:
time: 72.7 us; the launch traced here: 72.5 us
  Pallas kernels  68.5 us (94%)
  local copies, waits for them, and re-layouts  3.37 us (5%)
    pallas_call x1, Pallas kernels, body(): pl.pallas_call(functools.partial(kernel, n_blk, n_scene, group), out_shap...  68.5 us
    unnamed x1, local copies, waits for them, and re-layouts  1.87 us
    pallas_call x1, local copies, waits for them, and re-layouts, body(): pl.pallas_call(functools.partial(kernel, n_blk, n_scene, group), out_shap...  1.5 us

profile of v1, /device:TPU:1, one launch (start us, length us, event | category | flops | bytes accessed | tf_op | source)
XLA Modules:
  0.0 72.5 jit_solution(3184732859543226783)
XLA Ops:
  0.6 68.5 %decoder_level.1 = (bf16[1,4,512,128]{3,2,1,0:T(8,128)(2,1)}, f32[4,27,128]{2,1,0:T(8,128)}) custom-call(bf16[1,4,64,256]{3,2,1,0:T(8,128)(2,1)} %feat.1, s32[1,4,4]{2,1,0:T(4,128)} %coarse_nbr.1, s32[1,4]{1,0:T(1,128)} %dest.1, s32[1,4,4]{2,1,0:T(4,128)} %fine_nbr.1, bf16[1,4,512,128]{3,2,1,0:T(8,128)(2,1)} %skip.1, bf16[1,4,512,128]{3,2,1,0:T(8,128)(2,1)} %cot.1, ...), custom_call_target="tpu_custom_call" | custom-call | tf_op jit(solution)/shard_map/decoder_level/pallas_call | solution.py:639
  69.1 1.5 %copy.15 = f32[4,27,128]{2,0,1:T(4,128)} copy(f32[4,27,128]{2,1,0:T(8,128)} %get-tuple-element.3) | data formatting | bytes 110592 | tf_op jit(solution)/shard_map/decoder_level/pallas_call | solution.py:639
  70.6 1.9 %copy.17 = bf16[1,4,512,128]{3,2,1,0:T(8,128)(2,1)} copy(bf16[1,4,512,128]{3,2,1,0:T(8,128)(2,1)} %get-tuple-element.6) | data formatting | bytes 1048576

commit v2 on v1

--- a/solution.py
+++ b/solution.py
@@ -70,7 +70,7 @@
     double_z,
     order_g,
     out,
-    grad,
+    done,
     ext,
     wc,
     wu,
@@ -101,7 +101,6 @@
     shard_src,
     shards,
     done_src,
-    done,
     local_sem,
     halo_send,
     halo_recv,
@@ -184,7 +183,8 @@
         )
         return carry
 
-    lax.fori_loop(1, n_blk, greet_blk, 0)
+    for k in range(1, n_blk):
+        greet_blk(k, 0)
     lax.fori_loop(1, n_scene, greet_scene, 0)
 
     message_row = lax.broadcasted_iota(jnp.int32, (16, CF), 0)
@@ -220,7 +220,8 @@
             action(line, line * stride + odd)
             return carry
 
-        lax.fori_loop(0, LINES, step, 0)
+        for k in range(LINES):
+            step(k, 0)
 
     def meta_copy(line, peer):
         return remote(meta_src, meta.at[me], meta_send.at[line], meta_recv, blk=peer)
@@ -257,8 +258,6 @@
     faces_left = remote(
         own_faces, faces.at[pl.ds(2 * BLOCKS, BLOCKS)], halo_send.at[3], halo_recv.at[3], blk=left
     )
-    faces_right.start()
-    faces_left.start()
 
     first = (me - 1) * BLOCKS
     last_slot = 3 * BLOCKS - 1
@@ -328,6 +327,8 @@
             line_copy(line, peer).start()
 
     over_lines(send_line)
+    faces_right.start()
+    faces_left.start()
 
     total = n_blk * 16
     my_line = me // stride
@@ -361,7 +362,8 @@
             owner_copy(lax.rem(me + k, n_blk)).start()
             return carry
 
-        lax.fori_loop(1, n_blk, step, 0)
+        for k in range(1, n_blk):
+            step(k, 0)
 
     load_double.wait()
     load_wf.wait()
@@ -376,7 +378,8 @@
         ).reshape(12, 8, CF)
         return carry
 
-    lax.fori_loop(0, LINES, double_lines, 0)
+    for k in range(LINES):
+        double_lines(k, 0)
 
     def fine_block(b, carry):
         def beside(face):
@@ -429,7 +432,8 @@
         delta_t[b] = delta.T.astype(BF16)
         return carry
 
-    lax.fori_loop(0, BLOCKS, fine_block, 0)
+    for b in range(BLOCKS):
+        fine_block(b, 0)
     write_out = pltpu.make_async_copy(out_v, out.at[0], out_sem)
     write_out.start()
 
@@ -511,7 +515,8 @@
         shard_copy(k).start()
         return carry
 
-    lax.fori_loop(1, n_blk, send_shard, 0)
+    for k in range(1, n_blk):
+        send_shard(k, 0)
     pltpu.make_async_copy(shards, shards, shard_recv).wait()
     done_src[...] = jnp.sum(shards[...].astype(F32), axis=0)
 
@@ -525,17 +530,9 @@
         done_copy(k).start()
         return carry
 
-    lax.fori_loop(1, n_scene, send_done, 0)
+    for k in range(1, n_scene):
+        send_done(k, 0)
     pltpu.make_async_copy(done, done, done_recv).wait()
-    for index in range(n_scene):
-        count = min(group, TAPS - index * group)
-        if count <= 0:
-            continue
-        for channel in range(CF // n_blk):
-            grad[channel, index * group : index * group + count, :] = done[
-                index, channel * group : channel * group + count, :
-            ]
-
     feat_right.wait_send()
     feat_left.wait_send()
     faces_right.wait_send()
@@ -555,7 +552,8 @@
             owner_copy(lax.rem(me + k, n_blk)).wait_send()
             return carry
 
-        lax.fori_loop(1, n_blk, step, 0)
+        for k in range(1, n_blk):
+            step(k, 0)
 
     for k in range(rows):
         pair_copy(k).wait_send()
@@ -574,6 +572,32 @@
 
     lax.fori_loop(1, n_scene, sent_done, 0)
     write_out.wait()
+
+
+def assemble(group, level_out, shares, out, grad, shares_v, out_v, grad_v, in_sem, out_sem, grad_sem):
+    load = pltpu.make_async_copy(shares, shares_v, grad_sem.at[0])
+    reads = [
+        pltpu.make_async_copy(level_out.at[0, b], out_v.at[b], in_sem.at[b])
+        for b in range(BLOCKS)
+    ]
+    writes = [
+        pltpu.make_async_copy(out_v.at[b], out.at[0, b], out_sem.at[b]) for b in range(BLOCKS)
+    ]
+    load.start()
+    for read in reads:
+        read.start()
+    load.wait()
+    for tap in range(TAPS):
+        for channel in range(grad_v.shape[1]):
+            grad_v[tap, channel, :] = shares_v[tap // group, channel * group + tap % group, :]
+    store = pltpu.make_async_copy(grad_v, grad, grad_sem.at[1])
+    store.start()
+    for read, write in zip(reads, writes):
+        read.wait()
+        write.start()
+    store.wait()
+    for write in writes:
+        write.wait()
 
 
 def body(n_blk, n_scene, feat, coarse_nbr, dest, fine_nbr, skip, cot, w_coarse, w_up, w_fine):
@@ -582,7 +606,6 @@
     rows = n_scene // 2
     any_spec = pl.BlockSpec(memory_space=pl.ANY)
     smem_spec = pl.BlockSpec(memory_space=pltpu.SMEM)
-    vmem_spec = pl.BlockSpec(memory_space=pltpu.VMEM)
     vmem = pltpu.VMEM
     dma = pltpu.SemaphoreType.DMA
     scratch = [
@@ -616,7 +639,6 @@
         vmem((n_blk, shard * group, CF), BF16),
         vmem((n_blk, shard * group, CF), BF16),
         vmem((shard * group, CF), F32),
-        vmem((n_scene, shard * group, CF), F32),
         dma((10,)),
         dma((4,)),
         dma((4,)),
@@ -636,14 +658,14 @@
         dma,
         dma,
     ]
-    fine_out, gradient = pl.pallas_call(
+    level_out, shares = pl.pallas_call(
         functools.partial(kernel, n_blk, n_scene, group),
         out_shape=(
             jax.ShapeDtypeStruct((1, BLOCKS, 512, CF), BF16),
-            jax.ShapeDtypeStruct((shard, TAPS, CF), F32),
+            jax.ShapeDtypeStruct((n_scene, shard * group, CF), F32),
         ),
         in_specs=[any_spec, smem_spec, smem_spec, smem_spec] + [any_spec] * 9,
-        out_specs=(any_spec, vmem_spec),
+        out_specs=(any_spec, any_spec),
         scratch_shapes=scratch,
         compiler_params=pltpu.CompilerParams(
             collective_id=0, has_side_effects=True, vmem_limit_bytes=60 * 1024 * 1024
@@ -664,7 +686,25 @@
         jnp.asarray(doubled_rows(), BF16),
         jnp.asarray(shard_order(group), BF16),
     )
-    return fine_out, gradient
+    fine_out, gradient = pl.pallas_call(
+        functools.partial(assemble, group),
+        out_shape=(
+            jax.ShapeDtypeStruct((1, BLOCKS, 512, CF), BF16),
+            jax.ShapeDtypeStruct((TAPS, shard, CF), F32),
+        ),
+        in_specs=[any_spec, any_spec],
+        out_specs=(any_spec, any_spec),
+        scratch_shapes=[
+            vmem((n_scene, shard * group, CF), F32),
+            vmem((BLOCKS, 512, CF), BF16),
+            vmem((TAPS, shard, CF), F32),
+            dma((BLOCKS,)),
+            dma((BLOCKS,)),
+            dma((2,)),
+        ],
+        name="assemble",
+    )(level_out, shares)
+    return fine_out, jnp.transpose(gradient, (1, 0, 2))
 
 
 def solution(mesh):

time: 72.7 us -> 66.9 us (0.920)
  local copies, waits for them, and re-layouts: 3.37 us -> 0 us
  Pallas kernels: 68.5 us -> 66.1 us
    pallas_call x1, Pallas kernels: 68.5 us -> 64.2 us  [body(): pl.pallas_call(functools.partial(kernel, n_blk, n_scene, group), out_shap...]
    pallas_call x0 -> x1, Pallas kernels: none -> 1.95 us  [body(): pl.pallas_call(functools.partial(assemble, group), out_shape=(jax.ShapeDt...]
    unnamed x1 -> x0, local copies, waits for them, and re-layouts: 1.87 us -> none
    pallas_call x1 -> x0, local copies, waits for them, and re-layouts: 1.5 us -> none  [body(): pl.pallas_call(functools.partial(kernel, n_blk, n_scene, group), out_shap...]
where the time goes in v2:
time: 66.9 us; the launch traced here: 66.8 us
  Pallas kernels  66.1 us (99%)
    pallas_call x1, Pallas kernels, body(): pl.pallas_call(functools.partial(kernel, n_blk, n_scene, group), out_shap...  64.2 us
    pallas_call x1, Pallas kernels, body(): pl.pallas_call(functools.partial(assemble, group), out_shape=(jax.ShapeDt...  1.95 us

profile of v2, /device:TPU:1, one launch (start us, length us, event | category | flops | bytes accessed | tf_op | source)
XLA Modules:
  0.0 66.8 jit_solution(15192252470129007929)
XLA Ops:
  0.6 64.2 %decoder_level.1 = (bf16[1,4,512,128]{3,2,1,0:T(8,128)(2,1)}, f32[8,16,128]{2,1,0:T(8,128)}) custom-call(bf16[1,4,64,256]{3,2,1,0:T(8,128)(2,1)} %feat.1, s32[1,4,4]{2,1,0:T(4,128)} %coarse_nbr.1, s32[1,4]{1,0:T(1,128)} %dest.1, s32[1,4,4]{2,1,0:T(4,128)} %fine_nbr.1, bf16[1,4,512,128]{3,2,1,0:T(8,128)(2,1)} %skip.1, bf16[1,4,512,128]{3,2,1,0:T(8,128)(2,1)} %cot.1, ...), custom_call_target="tpu_custom_call" | custom-call | tf_op jit(solution)/shard_map/decoder_level/pallas_call | solution.py:661
  64.8 2.0 %assemble.1 = (bf16[1,4,512,128]{3,2,1,0:T(8,128)(2,1)}, f32[27,4,128]{2,1,0:T(4,128)}) custom-call(bf16[1,4,512,128]{3,2,1,0:T(8,128)(2,1)} %get-tuple-element.6.level_out, f32[8,16,128]{2,1,0:T(8,128)} %get-tuple-element.7.shares), custom_call_target="tpu_custom_call" | custom-call | tf_op jit(solution)/shard_map/assemble/pallas_call | solution.py:689

commit v3 on v2

--- a/solution.py
+++ b/solution.py
@@ -12,6 +12,8 @@
 BLOCKS = 4
 LINES = 16
 TAPS = 27
+DEPTH = 8
+REST = 48
 CF = 128
 CC = 256
 BF16 = jnp.bfloat16
@@ -92,12 +94,15 @@
     up,
     faces,
     cols,
+    deltas,
     delta_t,
     out_v,
+    rest,
+    own,
     pair_src,
     pair_dst,
-    y_src,
-    y_dst,
+    plane_src,
+    plane_dst,
     shard_src,
     shards,
     done_src,
@@ -112,19 +117,22 @@
     got_recv,
     pair_send,
     pair_recv,
-    y_send,
-    y_recv,
+    plane_send,
+    plane_recv,
     shard_send,
     shard_recv,
     done_send,
     done_recv,
     out_sem,
+    round_sem,
 ):
     me = lax.axis_index("blk")
     scene = lax.axis_index("scene")
     core = lax.rem(scene, 2)
     row = scene // 2
     rows = n_scene // 2
+    n_x, n_z = n_blk // DEPTH, DEPTH
+    my_x, my_z = me // n_z, lax.rem(me, n_z)
     stride = n_blk // LINES
     odd = lax.rem(scene, stride)
     right = lax.rem(me + 1, n_blk)
@@ -165,27 +173,31 @@
 
     barrier = pltpu.get_barrier_semaphore()
 
-    def greet_blk(k, carry):
-        pl.semaphore_signal(
-            barrier,
-            inc=1,
-            device_id={"blk": lax.rem(me + k, n_blk)},
-            device_id_type=MESH,
-        )
-        return carry
-
-    def greet_scene(k, carry):
-        pl.semaphore_signal(
-            barrier,
-            inc=1,
-            device_id={"scene": lax.rem(scene + k, n_scene)},
-            device_id_type=MESH,
-        )
-        return carry
-
-    for k in range(1, n_blk):
-        greet_blk(k, 0)
-    lax.fori_loop(1, n_scene, greet_scene, 0)
+    def along(x=0, y=0, z=0, c=0):
+        return {
+            "blk": lax.rem(my_x + x, n_x) * n_z + lax.rem(my_z + z, n_z),
+            "scene": 2 * lax.rem(row + y, rows) + lax.rem(core + c, 2),
+        }
+
+    def greet(semaphore, places):
+        for place in places:
+            pl.semaphore_signal(semaphore, inc=1, device_id=place, device_id_type=MESH)
+
+    beside_me = [
+        along(z=1),
+        along(z=n_z - 1),
+        along(x=1),
+        along(x=n_x - 1),
+        along(y=1),
+        along(y=rows - 1),
+    ]
+    first_round = [{"blk": right}, {"blk": left}, along(c=1)] + beside_me
+    later_rounds = [
+        beside_me,
+        [along(z=2), along(z=n_z - 2), along(c=1)],
+        [along(x=x) for x in range(1, n_x)] + [along(y=y) for y in range(1, rows)],
+    ]
+    greet(barrier, first_round)
 
     message_row = lax.broadcasted_iota(jnp.int32, (16, CF), 0)
     owner_rows = lax.rem(message_row, 4)
@@ -193,7 +205,7 @@
         owner_rows = owner_rows + jnp.where(message_row // 4 == b, 4 * dest[0, b], 0)
     meta_src[...] = owner_rows
 
-    pl.semaphore_wait(barrier, n_blk + n_scene - 2)
+    pl.semaphore_wait(barrier, len(first_round))
 
     def remote(source, target, send, recv, **where):
         return pltpu.make_async_remote_copy(
@@ -213,6 +225,9 @@
     )
     feat_right.start()
     feat_left.start()
+    for index, places in enumerate(later_rounds):
+        greet(round_sem.at[index], places)
+        pl.semaphore_wait(round_sem.at[index], len(places))
 
     def over_lines(action):
         def step(k, carry):
@@ -414,11 +429,11 @@
             )
             for q in range(3):
                 for r in range(3):
-                    cols[3 * q + r, b, px] = shifted[r][q : q + 8].reshape(64, CF).astype(BF16)
+                    cols[3 * q + r, b // 2, px, b % 2] = shifted[r][q : q + 8].reshape(64, CF).astype(BF16)
         pre = None
         for p in range(3):
             left_side = jnp.concatenate(
-                [cols[qr, b, p : p + 8].reshape(512, CF) for qr in range(9)], axis=1
+                [cols[qr, b // 2, p : p + 8, b % 2].reshape(512, CF) for qr in range(9)], axis=1
             )
             product = jnp.dot(
                 left_side,
@@ -429,7 +444,7 @@
         sigma = 1.0 / (1.0 + jnp.exp(-pre))
         out_v[b] = (pre * sigma).astype(BF16)
         delta = cot_v[b].astype(F32) * (sigma * (1.0 + pre * (1.0 - sigma)))
-        delta_t[b] = delta.T.astype(BF16)
+        deltas[b // 2, :, b % 2] = delta.reshape(8, 64, CF)
         return carry
 
     for b in range(BLOCKS):
@@ -437,22 +452,25 @@
     write_out = pltpu.make_async_copy(out_v, out.at[0], out_sem)
     write_out.start()
 
-    def group_terms(index):
-        pairs = []
-        for first_tap in range(0, group, 2):
-            picked = []
-            for tap in (first_tap, first_tap + 1):
-                which = lax.rem(index * group + tap, TAPS)
-                picked.append((which // 9, lax.rem(which, 9)))
-            terms = None
-            for b in range(BLOCKS):
-                sides = jnp.concatenate(
-                    [cols[qr, b, pl.ds(p, 8)].reshape(512, CF) for p, qr in picked], axis=1
-                )
-                product = jnp.dot(delta_t[b], sides, preferred_element_type=F32)
-                terms = product if terms is None else terms + product
-            pairs.append(terms)
-        return jnp.concatenate(pairs, axis=1)
+    for half in range(BLOCKS // 2):
+        turned = deltas[half].reshape(1024, CF).T.astype(BF16)
+        for p in range(3):
+            rows_p = slice(CF * p, CF * (p + 1))
+            if p > 0:
+                delta_t[half, rows_p, : CF * p] = jnp.zeros((CF, CF * p), BF16)
+            delta_t[half, rows_p, CF * p : CF * p + 1024] = turned
+            if p < 2:
+                delta_t[half, rows_p, CF * p + 1024 :] = jnp.zeros((CF, CF * (2 - p)), BF16)
+
+    def terms_of(first, count):
+        terms = None
+        for half in range(BLOCKS // 2):
+            sides = jnp.concatenate(
+                [cols[first + j, half].reshape(1280, CF) for j in range(count)], axis=1
+            )
+            product = jnp.dot(delta_t[half], sides, preferred_element_type=F32)
+            terms = product if terms is None else terms + product
+        return terms
 
     def pair_copy(k):
         return remote(
@@ -463,60 +481,73 @@
             scene=scene + 1 - 2 * core,
         )
 
-    def y_copy(k):
+    load_gorder.wait()
+
+    def plane_copy(k, j):
+        peer_x = lax.rem(my_x + 1 + j, n_x)
+        source = plane_src.at[k, pl.ds(pl.multiple_of(CF * peer_x, CF), CF)]
+        target = plane_dst.at[my_x * rows + row]
+        if k == rows - 1 and j == n_x - 1:
+            return pltpu.make_async_copy(source, target, plane_recv)
         return remote(
-            y_src.at[k],
-            y_dst.at[k],
-            y_send.at[k],
-            y_recv.at[k],
+            source,
+            target,
+            plane_send.at[k * n_x + j],
+            plane_recv,
+            blk=peer_x * n_z + my_z,
             scene=2 * lax.rem(row + 1 + k, rows) + core,
         )
 
-    def for_partner(k, carry):
-        pair_src[k] = group_terms(2 * lax.rem(row + 1 + k, rows) + 1 - core).astype(BF16)
+    def send_plane(k):
+        pair_copy(k).wait_recv()
+        total_k = (own[k] + pair_dst[k].astype(F32)).astype(BF16)
+        filled = jnp.concatenate([total_k[3 * CF :], jnp.zeros((CF - REST, CF), BF16)], axis=0)
+        parts = [total_k[CF * p : CF * (p + 1)] for p in range(3)] + [filled]
+        ordered = lax.dot_general(
+            order_gv[...],
+            jnp.concatenate(parts, axis=1),
+            (((1,), (1,)), ((), ())),
+            preferred_element_type=F32,
+        )
+        plane_src[k] = ordered.astype(BF16)
+        for j in range(n_x):
+            plane_copy(k, j).start()
+
+    rest[...] = terms_of(8, 1)
+    for k in range(rows):
+        target = lax.rem(row + 1 + k, rows)
+        terms = terms_of(2 * target, 2)
+        low, high = terms[:, :CF], terms[:, CF:]
+
+        def rest_of(member):
+            return rest[pl.ds(pl.multiple_of(REST * member, 16), REST), :]
+
+        pair_src[k, : 3 * CF] = jnp.where(core == 0, high, low).astype(BF16)
+        pair_src[k, 3 * CF :] = rest_of(2 * target + 1 - core).astype(BF16)
         pair_copy(k).start()
-        return carry
-
-    lax.fori_loop(0, rows, for_partner, 0)
-
-    def pair_sum(k):
-        terms = group_terms(2 * lax.rem(row + 1 + k, rows) + core)
-        pair_copy(k).wait_recv()
-        return terms + pair_dst[k].astype(F32)
-
-    def for_row(k, carry):
-        y_src[k] = pair_sum(k).astype(BF16)
-        y_copy(k).start()
-        return carry
-
-    lax.fori_loop(0, rows - 1, for_row, 0)
-    scene_sum = pair_sum(rows - 1)
-    for k in range(rows - 1):
-        y_copy(k).wait_recv()
-        scene_sum = scene_sum + y_dst[k].astype(F32)
-    load_gorder.wait()
-    ordered = lax.dot_general(
-        order_gv[...],
-        scene_sum.astype(BF16),
-        (((1,), (1,)), ((), ())),
-        preferred_element_type=F32,
-    )
-    shard_src[...] = ordered.astype(BF16).reshape(shard_src.shape)
+        own[k, : 3 * CF] = jnp.where(core == 0, low, high)
+        own[k, 3 * CF :] = rest_of(2 * target + core)
+        if k > 1:
+            send_plane(k - 2)
+    send_plane(rows - 2)
+    send_plane(rows - 1)
+    pltpu.make_async_copy(plane_dst, plane_dst, plane_recv).wait()
+    plane_sum = jnp.sum(plane_dst[...].astype(F32), axis=0)
+    shard_src[...] = plane_sum.astype(BF16).reshape(shard_src.shape)
 
     def shard_copy(k):
-        peer = lax.rem(me + k, n_blk)
+        peer = lax.rem(my_z + k, n_z)
         return remote(
-            shard_src.at[peer], shards.at[me], shard_send.at[peer], shard_recv, blk=peer
-        )
-
-    pltpu.make_async_copy(shard_src.at[me], shards.at[me], shard_recv).start()
-
-    def send_shard(k, carry):
+            shard_src.at[peer],
+            shards.at[my_z],
+            shard_send.at[peer],
+            shard_recv,
+            blk=my_x * n_z + peer,
+        )
+
+    for k in range(1, n_z):
         shard_copy(k).start()
-        return carry
-
-    for k in range(1, n_blk):
-        send_shard(k, 0)
+    pltpu.make_async_copy(shard_src.at[my_z], shards.at[my_z], shard_recv).start()
     pltpu.make_async_copy(shards, shards, shard_recv).wait()
     done_src[...] = jnp.sum(shards[...].astype(F32), axis=0)
 
@@ -557,14 +588,12 @@
 
     for k in range(rows):
         pair_copy(k).wait_send()
-    for k in range(rows - 1):
-        y_copy(k).wait_send()
-
-    def sent_shard(k, carry):
+    for k in range(rows):
+        for j in range(n_x):
+            if k < rows - 1 or j < n_x - 1:
+                plane_copy(k, j).wait_send()
+    for k in range(1, n_z):
         shard_copy(k).wait_send()
-        return carry
-
-    lax.fori_loop(1, n_blk, sent_shard, 0)
 
     def sent_done(k, carry):
         done_copy(k).wait_send()
@@ -587,9 +616,17 @@
     for read in reads:
         read.start()
     load.wait()
-    for tap in range(TAPS):
-        for channel in range(grad_v.shape[1]):
-            grad_v[tap, channel, :] = shares_v[tap // group, channel * group + tap % group, :]
+    n_scene = shares_v.shape[0]
+    for channel in range(grad_v.shape[1]):
+        for p in range(3):
+            for qr in range(n_scene):
+                grad_v[9 * p + qr, channel, :] = shares_v[qr, channel * group + p, :]
+        at = channel * group + 3
+        last = jnp.concatenate(
+            [shares_v[s, at : at + 1, :REST] for s in range(n_scene)], axis=1
+        )
+        for p in range(3):
+            grad_v[9 * p + 8, channel : channel + 1, :] = last[:, CF * p : CF * (p + 1)]
     store = pltpu.make_async_copy(grad_v, grad, grad_sem.at[1])
     store.start()
     for read, write in zip(reads, writes):
@@ -601,9 +638,10 @@
 
 
 def body(n_blk, n_scene, feat, coarse_nbr, dest, fine_nbr, skip, cot, w_coarse, w_up, w_fine):
-    group = 4 * -(-TAPS // (4 * n_scene))
+    group = 4
     shard = CF // n_blk
     rows = n_scene // 2
+    n_x = n_blk // DEPTH
     any_spec = pl.BlockSpec(memory_space=pl.ANY)
     smem_spec = pl.BlockSpec(memory_space=pltpu.SMEM)
     vmem = pltpu.VMEM
@@ -629,15 +667,18 @@
         vmem((LINES, 48, CF), BF16),
         vmem((LINES, 12, 8, CF), F32),
         vmem((3 * BLOCKS, 4, 64, CF), BF16),
-        vmem((9, BLOCKS, 10, 64, CF), BF16),
-        vmem((BLOCKS, CF, 512), BF16),
+        vmem((9, BLOCKS // 2, 10, 2, 64, CF), BF16),
+        vmem((BLOCKS // 2, 8, 2, 64, CF), F32),
+        vmem((BLOCKS // 2, 3 * CF, 1280), BF16),
         vmem((BLOCKS, 512, CF), BF16),
-        vmem((rows, CF, group * CF), BF16),
-        vmem((rows, CF, group * CF), BF16),
-        vmem((max(rows - 1, 1), CF, group * CF), BF16),
-        vmem((max(rows - 1, 1), CF, group * CF), BF16),
-        vmem((n_blk, shard * group, CF), BF16),
-        vmem((n_blk, shard * group, CF), BF16),
+        vmem((3 * CF, CF), F32),
+        vmem((rows, 3 * CF + REST, CF), F32),
+        vmem((rows, 3 * CF + REST, CF), BF16),
+        vmem((rows, 3 * CF + REST, CF), BF16),
+        vmem((rows, group * CF, CF), BF16),
+        vmem((rows * n_x, group * CF // n_x, CF), BF16),
+        vmem((DEPTH, shard * group, CF), BF16),
+        vmem((DEPTH, shard * group, CF), BF16),
         vmem((shard * group, CF), F32),
         dma((10,)),
         dma((4,)),
@@ -650,13 +691,14 @@
         dma,
         dma((rows,)),
         dma((rows,)),
-        dma((max(rows - 1, 1),)),
-        dma((max(rows - 1, 1),)),
-        dma((n_blk,)),
+        dma((rows * n_x,)),
+        dma,
+        dma((DEPTH,)),
         dma,
         dma((n_scene,)),
         dma,
         dma,
+        pltpu.SemaphoreType.REGULAR((3,)),
     ]
     level_out, shares = pl.pallas_call(
         functools.partial(kernel, n_blk, n_scene, group),

time: 66.9 us -> 64.1 us (0.958)
  Pallas kernels: 66.1 us -> 63.3 us
    pallas_call x1, Pallas kernels: 64.2 us -> 61.3 us  [body(): pl.pallas_call(functools.partial(kernel, n_blk, n_scene, group), out_shap...]
where the time goes in v3:
time: 64.1 us; the launch traced here: 63.9 us
  Pallas kernels  63.3 us (99%)
    pallas_call x1, Pallas kernels, body(): pl.pallas_call(functools.partial(kernel, n_blk, n_scene, group), out_shap...  61.3 us
    pallas_call x1, Pallas kernels, body(): pl.pallas_call(functools.partial(assemble, group), out_shape=(jax.ShapeDt...  2.01 us

profile of v3, /device:TPU:1, one launch (start us, length us, event | category | flops | bytes accessed | tf_op | source)
XLA Modules:
  0.0 63.9 jit_solution(2471631239352122105)
XLA Ops:
  0.6 61.3 %decoder_level.1 = (bf16[1,4,512,128]{3,2,1,0:T(8,128)(2,1)}, f32[8,16,128]{2,1,0:T(8,128)}) custom-call(bf16[1,4,64,256]{3,2,1,0:T(8,128)(2,1)} %feat.1, s32[1,4,4]{2,1,0:T(4,128)} %coarse_nbr.1, s32[1,4]{1,0:T(1,128)} %dest.1, s32[1,4,4]{2,1,0:T(4,128)} %fine_nbr.1, bf16[1,4,512,128]{3,2,1,0:T(8,128)(2,1)} %skip.1, bf16[1,4,512,128]{3,2,1,0:T(8,128)(2,1)} %cot.1, ...), custom_call_target="tpu_custom_call" | custom-call | tf_op jit(solution)/shard_map/decoder_level/pallas_call | solution.py:703
  61.9 2.0 %assemble.1 = (bf16[1,4,512,128]{3,2,1,0:T(8,128)(2,1)}, f32[27,4,128]{2,1,0:T(4,128)}) custom-call(bf16[1,4,512,128]{3,2,1,0:T(8,128)(2,1)} %get-tuple-element.6.level_out, f32[8,16,128]{2,1,0:T(8,128)} %get-tuple-element.7.shares), custom_call_target="tpu_custom_call" | custom-call | tf_op jit(solution)/shard_map/assemble/pallas_call | solution.py:731

commit v4 on v3

--- a/solution.py
+++ b/solution.py
@@ -59,9 +59,9 @@
     n_scene,
     group,
     feat,
-    coarse_nbr,
-    dest,
-    fine_nbr,
+    coarse_nbr_in,
+    dest_in,
+    fine_nbr_in,
     skip,
     cot,
     w_coarse,
@@ -73,6 +73,9 @@
     order_g,
     out,
     done,
+    coarse_nbr,
+    dest,
+    fine_nbr,
     ext,
     wc,
     wu,
@@ -139,38 +142,6 @@
     left = lax.rem(me + n_blk - 1, n_blk)
     is_mid = lax.rem(me, stride) == odd
 
-    loads = [
-        pltpu.make_async_copy(source, target, local_sem.at[index])
-        for index, (source, target) in enumerate(
-            (
-                (feat.at[0], ext.at[pl.ds(BLOCKS, BLOCKS)]),
-                (skip.at[0], skip_v),
-                (sel_c, sel_cv),
-                (w_coarse, wc),
-                (w_up, wu),
-                (order_c, order_cv),
-                (double_z, double_v),
-                (w_fine, wf),
-                (cot.at[0], cot_v),
-                (order_g, order_gv),
-            )
-        )
-    ]
-    for load in loads:
-        load.start()
-    (
-        load_feat,
-        load_skip,
-        load_sel,
-        load_wc,
-        load_wu,
-        load_order,
-        load_double,
-        load_wf,
-        load_cot,
-        load_gorder,
-    ) = loads
-
     barrier = pltpu.get_barrier_semaphore()
 
     def along(x=0, y=0, z=0, c=0):
@@ -199,11 +170,43 @@
     ]
     greet(barrier, first_round)
 
-    message_row = lax.broadcasted_iota(jnp.int32, (16, CF), 0)
-    owner_rows = lax.rem(message_row, 4)
-    for b in range(BLOCKS):
-        owner_rows = owner_rows + jnp.where(message_row // 4 == b, 4 * dest[0, b], 0)
-    meta_src[...] = owner_rows
+    loads = [
+        pltpu.make_async_copy(source, target, local_sem.at[index])
+        for index, (source, target) in enumerate(
+            (
+                (feat.at[0], ext.at[pl.ds(BLOCKS, BLOCKS)]),
+                (skip.at[0], skip_v),
+                (sel_c, sel_cv),
+                (w_coarse, wc),
+                (w_up, wu),
+                (order_c, order_cv),
+                (double_z, double_v),
+                (w_fine, wf),
+                (cot.at[0], cot_v),
+                (order_g, order_gv),
+                (dest_in, dest),
+                (coarse_nbr_in, coarse_nbr),
+                (fine_nbr_in, fine_nbr),
+            )
+        )
+    ]
+    for load in loads:
+        load.start()
+    (
+        load_feat,
+        load_skip,
+        load_sel,
+        load_wc,
+        load_wu,
+        load_order,
+        load_double,
+        load_wf,
+        load_cot,
+        load_gorder,
+        load_dest,
+        load_coarse_nbr,
+        load_fine_nbr,
+    ) = loads
 
     pl.semaphore_wait(barrier, len(first_round))
 
@@ -229,14 +232,21 @@
         greet(round_sem.at[index], places)
         pl.semaphore_wait(round_sem.at[index], len(places))
 
+    load_dest.wait()
+    message_row = lax.broadcasted_iota(jnp.int32, (16, CF), 0)
+    owner_rows = lax.rem(message_row, 4)
+    for b in range(BLOCKS):
+        owner_rows = owner_rows + jnp.where(message_row // 4 == b, 4 * dest[0, b], 0)
+    meta_src[...] = owner_rows
+
+    far_x, far_z = (2, 1, 3, 0), (4, 3, 5, 2, 6, 1, 7, 0)
+    base_z = my_z + lax.rem(my_z + odd, stride)
+
     def over_lines(action):
-        def step(k, carry):
-            line = lax.rem(me // stride + k, LINES)
-            action(line, line * stride + odd)
-            return carry
-
-        for k in range(LINES):
-            step(k, 0)
+        for dx in far_x:
+            for dz in (4, 2, 6, 0):
+                peer = lax.rem(my_x + dx, n_x) * n_z + lax.rem(base_z + dz, n_z)
+                action(peer // stride, peer)
 
     def meta_copy(line, peer):
         return remote(meta_src, meta.at[me], meta_send.at[line], meta_recv, blk=peer)
@@ -278,6 +288,7 @@
     last_slot = 3 * BLOCKS - 1
     load_feat.wait()
     load_sel.wait()
+    load_coarse_nbr.wait()
     feat_right.wait_recv()
     feat_left.wait_recv()
 
@@ -342,8 +353,6 @@
             line_copy(line, peer).start()
 
     over_lines(send_line)
-    faces_right.start()
-    faces_left.start()
 
     total = n_blk * 16
     my_line = me // stride
@@ -373,14 +382,16 @@
         ).astype(BF16)
         pltpu.make_async_copy(perm.at[pl.ds(16 * me, 48)], got.at[my_line], got_recv).start()
 
-        def step(k, carry):
-            owner_copy(lax.rem(me + k, n_blk)).start()
-            return carry
-
-        for k in range(1, n_blk):
-            step(k, 0)
-
+        for dx in far_x:
+            for dz in far_z:
+                if dx or dz:
+                    place = lax.rem(my_x + dx, n_x) * n_z + lax.rem(my_z + dz, n_z)
+                    owner_copy(place).start()
+
+    faces_right.start()
+    faces_left.start()
     load_double.wait()
+    load_fine_nbr.wait()
     load_wf.wait()
     load_cot.wait()
     faces_right.wait_recv()
@@ -484,7 +495,7 @@
     load_gorder.wait()
 
     def plane_copy(k, j):
-        peer_x = lax.rem(my_x + 1 + j, n_x)
+        peer_x = lax.rem(my_x + far_x[j], n_x)
         source = plane_src.at[k, pl.ds(pl.multiple_of(CF * peer_x, CF), CF)]
         target = plane_dst.at[my_x * rows + row]
         if k == rows - 1 and j == n_x - 1:
@@ -495,7 +506,7 @@
             plane_send.at[k * n_x + j],
             plane_recv,
             blk=peer_x * n_z + my_z,
-            scene=2 * lax.rem(row + 1 + k, rows) + core,
+            scene=2 * lax.rem(row + far_x[k], rows) + core,
         )
 
     def send_plane(k):
@@ -515,7 +526,7 @@
 
     rest[...] = terms_of(8, 1)
     for k in range(rows):
-        target = lax.rem(row + 1 + k, rows)
+        target = lax.rem(row + far_x[k], rows)
         terms = terms_of(2 * target, 2)
         low, high = terms[:, :CF], terms[:, CF:]
 
@@ -545,7 +556,7 @@
             blk=my_x * n_z + peer,
         )
 
-    for k in range(1, n_z):
+    for k in far_z[:-1]:
         shard_copy(k).start()
     pltpu.make_async_copy(shard_src.at[my_z], shards.at[my_z], shard_recv).start()
     pltpu.make_async_copy(shards, shards, shard_recv).wait()
@@ -561,7 +572,7 @@
         done_copy(k).start()
         return carry
 
-    for k in range(1, n_scene):
+    for k in (4, 5, 3, 2, 6, 7, 1):
         send_done(k, 0)
     pltpu.make_async_copy(done, done, done_recv).wait()
     feat_right.wait_send()
@@ -643,10 +654,12 @@
     rows = n_scene // 2
     n_x = n_blk // DEPTH
     any_spec = pl.BlockSpec(memory_space=pl.ANY)
-    smem_spec = pl.BlockSpec(memory_space=pltpu.SMEM)
     vmem = pltpu.VMEM
     dma = pltpu.SemaphoreType.DMA
     scratch = [
+        pltpu.SMEM((1, BLOCKS, 4), jnp.int32),
+        pltpu.SMEM((1, BLOCKS), jnp.int32),
+        pltpu.SMEM((1, BLOCKS, 4), jnp.int32),
         vmem((3 * BLOCKS, 64, CC), BF16),
         vmem((TAPS, CC, CC), BF16),
         vmem((CC, CF), BF16),
@@ -680,7 +693,7 @@
         vmem((DEPTH, shard * group, CF), BF16),
         vmem((DEPTH, shard * group, CF), BF16),
         vmem((shard * group, CF), F32),
-        dma((10,)),
+        dma((13,)),
         dma((4,)),
         dma((4,)),
         dma((LINES,)),
@@ -706,7 +719,7 @@
             jax.ShapeDtypeStruct((1, BLOCKS, 512, CF), BF16),
             jax.ShapeDtypeStruct((n_scene, shard * group, CF), F32),
         ),
-        in_specs=[any_spec, smem_spec, smem_spec, smem_spec] + [any_spec] * 9,
+        in_specs=[any_spec] * 13,
         out_specs=(any_spec, any_spec),
         scratch_shapes=scratch,
         compiler_params=pltpu.CompilerParams(

time: 64.1 us -> 61.8 us (0.964)
  Pallas kernels: 63.3 us -> 61 us
    pallas_call x1, Pallas kernels: 61.3 us -> 59 us  [body(): pl.pallas_call(functools.partial(kernel, n_blk, n_scene, group), out_shap...]
where the time goes in v4:
time: 61.8 us; the launch traced here: 61.7 us
  Pallas kernels  61 us (99%)
  between operations  0.64 us (1%)
    pallas_call x1, Pallas kernels, body(): pl.pallas_call(functools.partial(kernel, n_blk, n_scene, group), out_shap...  59 us
    pallas_call x1, Pallas kernels, body(): pl.pallas_call(functools.partial(assemble, group), out_shape=(jax.ShapeDt...  2.01 us

profile of v4, /device:TPU:1, one launch (start us, length us, event | category | flops | bytes accessed | tf_op | source)
XLA Modules:
  0.0 61.7 jit_solution(8475568347931044515)
XLA Ops:
  0.6 59.0 %decoder_level.1 = (bf16[1,4,512,128]{3,2,1,0:T(8,128)(2,1)}, f32[8,16,128]{2,1,0:T(8,128)}) custom-call(bf16[1,4,64,256]{3,2,1,0:T(8,128)(2,1)} %feat.1, s32[1,4,4]{2,1,0:T(4,128)} %coarse_nbr_in.1, s32[1,4]{1,0:T(1,128)} %dest_in.1, s32[1,4,4]{2,1,0:T(4,128)} %fine_nbr_in.1, bf16[1,4,512,128]{3,2,1,0:T(8,128)(2,1)} %skip.1, bf16[1,4,512,128]{3,2,1,0:T(8,128)(2,1)} %cot.1, ...), custom_call_target="tpu_custom_call" | custom-call | tf_op jit(solution)/shard_map/decoder_level/pallas_call | solution.py:716
  59.7 2.0 %assemble.1 = (bf16[1,4,512,128]{3,2,1,0:T(8,128)(2,1)}, f32[27,4,128]{2,1,0:T(4,128)}) custom-call(bf16[1,4,512,128]{3,2,1,0:T(8,128)(2,1)} %get-tuple-element.6.level_out, f32[8,16,128]{2,1,0:T(8,128)} %get-tuple-element.7.shares), custom_call_target="tpu_custom_call" | custom-call | tf_op jit(solution)/shard_map/assemble/pallas_call | solution.py:744
